TPU v7x, 128 devices: a whole 4x4x4 slice. The times are simulated.
128 devices in a mesh: row: 8 (over y_lo, x), rhs: 16 (over y_hi, z, core).
Axes of the slice: x: 4, y: 4 (y_hi: 2, y_lo: 2; y = y_hi * 2 + y_lo), z: 4, core: 2. Of those that a mesh axis runs over, the one named last changes fastest.
Arguments:
- factor: float32 [6144, 24, 256], P('row', None, 'rhs'), as said below
- inverses: float32 [24, 256, 256], P('row'), as said below
- right_side: float32 [6144, 8192], P('row', 'rhs'), may hold values from -6 to 6
Outputs:
- solution: float32 [6144, 8192], P('row', 'rhs')
Inputs may be any that keep to these rules, and one draw needn't show every extreme that they name: factor[i, j, c] is zero unless j is less than i // 256. Each inverses[p] is lower triangular with a positive diagonal.
All inputs are finite; a program needn't handle non-finite values.
Results may differ from a plain program's by a relative error of at most 0.0001.
Values sent between devices are 32-bit elements; how exact they have to be, the bound alone decides.
A program may use at most 128 MiB of HBM per device.

v0:
```python
import jax
import jax.numpy as jnp
from jax import lax
from jax.sharding import PartitionSpec as P


def from_root(block, axis, owner):
    block = jnp.where(lax.axis_index(axis) == owner, block, jnp.zeros_like(block))
    return lax.psum(block, axis)


def mult(left, right):
    return jnp.dot(left, right, preferred_element_type=jnp.float32, precision=lax.Precision.HIGHEST)


def body(factor, inverses, right_side):
    block = right_side.shape[0]
    panel = inverses.shape[1]
    per_block = inverses.shape[0]
    rounds = lax.axis_size("row")
    mine = lax.axis_index("row")
    gathered = lax.all_gather(factor, "rhs", axis=2, tiled=True)

    def fetch(first, count):
        return lax.dynamic_slice_in_dim(gathered, first, count, 1)

    def apply_tiles(residual, tiles, solved):
        return residual - mult(tiles.reshape(block, -1), solved)

    solution = jnp.zeros_like(right_side)

    def step_block(index, state):
        residual, solution = state
        tiles = fetch(index * per_block, per_block)
        working = residual
        pieces = []
        for inner in range(per_block):
            solved_part = mult(inverses[inner], working[inner * panel : (inner + 1) * panel])
            pieces.append(solved_part)
            working = working - mult(tiles[:, inner, :], solved_part)
        solved = from_root(jnp.concatenate(pieces, axis=0), "row", index)
        residual = apply_tiles(residual, tiles, solved)
        solution = jnp.where(mine == index, solved, solution)
        return (residual, solution)

    residual, solution = lax.fori_loop(0, rounds, step_block, (right_side, solution))
    return solution


def solution(mesh):
    placed = (P("row", None, "rhs"), P("row", None, None), P("row", "rhs"))
    return jax.shard_map(
        body, mesh=mesh, in_specs=placed, out_specs=P("row", "rhs"), check_vma=False
    )
```

profile of v0, /device:TPU:14, one launch (start us, length us, event | category | flops | bytes accessed | tf_op | source)
XLA Modules:
  0.0 901.7 jit_solution(14142752373888598711)
XLA Ops:
  7.3 123.0 %all-gather.2.cloned.1.call-done = f32[768,24,256]{0,2,1:T(8,128)} async-done(((f32[768,24,16]{0,2,1:T(8,128)}), f32[768,24,256]{0,2,1:T(8,128)}) %all-gather.2.cloned.1.call-update) | async-done | bytes 18874384 | tf_op jit(solution)/shard_map/all_gather | solution.py:22
  130.3 763.8 %while.16 = (s32[]{:T(128)}, f32[768,512]{1,0:T(8,128)S(1)}, f32[768,512]{1,0:T(8,128)S(1)}, f32[768,24,256]{0,2,1:T(8,128)}, f32[3,256,256]{2,1,0:T(8,128)}, /*...) while((s32[]{:T(128)}, f32[768,512]{1,0:T(8,128)S(1)}, ...), condition=%wide.region_2.3_spmd.clone, body=%wide.region_0.2_spmd.clone.sunk | while | flops 7251034112 | bytes 50332008 | solution.py:46
  139.7 3.2 constant_dynamic-slice_fusion.2
  143.0 73.2 %all-reduce.2.cloned.1.call-done = f32[768,512]{1,0:T(8,128)} async-done(((f32[768,512]{1,0:T(8,128)}), f32[768,512]{1,0:T(8,128)}) %all-reduce.2.cloned.1.call-update) | async-done | bytes 1572880 | tf_op jit(solution)/shard_map/while/body/eval_jaxpr/psum | solution.py:9
  216.2 6.4 convolution_subtract_fusion.5
  232.6 3.2 constant_dynamic-slice_fusion.2
  235.8 76.1 %all-reduce.2.cloned.1.call-done = f32[768,512]{1,0:T(8,128)} async-done(((f32[768,512]{1,0:T(8,128)}), f32[768,512]{1,0:T(8,128)}) %all-reduce.2.cloned.1.call-update) | async-done | bytes 1572880 | tf_op jit(solution)/shard_map/while/body/eval_jaxpr/psum | solution.py:9
  312.0 6.4 convolution_subtract_fusion.5
  328.5 3.2 constant_dynamic-slice_fusion.2
  331.7 76.2 %all-reduce.2.cloned.1.call-done = f32[768,512]{1,0:T(8,128)} async-done(((f32[768,512]{1,0:T(8,128)}), f32[768,512]{1,0:T(8,128)}) %all-reduce.2.cloned.1.call-update) | async-done | bytes 1572880 | tf_op jit(solution)/shard_map/while/body/eval_jaxpr/psum | solution.py:9
  407.8 6.4 convolution_subtract_fusion.5
  424.3 3.2 constant_dynamic-slice_fusion.2
  427.5 76.2 %all-reduce.2.cloned.1.call-done = f32[768,512]{1,0:T(8,128)} async-done(((f32[768,512]{1,0:T(8,128)}), f32[768,512]{1,0:T(8,128)}) %all-reduce.2.cloned.1.call-update) | async-done | bytes 1572880 | tf_op jit(solution)/shard_map/while/body/eval_jaxpr/psum | solution.py:9
  503.7 6.4 convolution_subtract_fusion.5
  520.2 3.2 constant_dynamic-slice_fusion.2
  523.4 76.2 %all-reduce.2.cloned.1.call-done = f32[768,512]{1,0:T(8,128)} async-done(((f32[768,512]{1,0:T(8,128)}), f32[768,512]{1,0:T(8,128)}) %all-reduce.2.cloned.1.call-update) | async-done | bytes 1572880 | tf_op jit(solution)/shard_map/while/body/eval_jaxpr/psum | solution.py:9
  599.6 6.4 convolution_subtract_fusion.5
  616.1 3.2 constant_dynamic-slice_fusion.2
  619.3 76.2 %all-reduce.2.cloned.1.call-done = f32[768,512]{1,0:T(8,128)} async-done(((f32[768,512]{1,0:T(8,128)}), f32[768,512]{1,0:T(8,128)}) %all-reduce.2.cloned.1.call-update) | async-done | bytes 1572880 | tf_op jit(solution)/shard_map/while/body/eval_jaxpr/psum | solution.py:9
  695.4 6.4 convolution_subtract_fusion.5
  715.1 76.1 %all-reduce.2.cloned.1.call-done = f32[768,512]{1,0:T(8,128)} async-done(((f32[768,512]{1,0:T(8,128)}), f32[768,512]{1,0:T(8,128)}) %all-reduce.2.cloned.1.call-update) | async-done | bytes 1572880 | tf_op jit(solution)/shard_map/while/body/eval_jaxpr/psum | solution.py:9
  791.3 6.4 convolution_subtract_fusion.5
  811.0 76.2 %all-reduce.2.cloned.1.call-done = f32[768,512]{1,0:T(8,128)} async-done(((f32[768,512]{1,0:T(8,128)}), f32[768,512]{1,0:T(8,128)}) %all-reduce.2.cloned.1.call-update) | async-done | bytes 1572880 | tf_op jit(solution)/shard_map/while/body/eval_jaxpr/psum | solution.py:9
  887.1 6.4 convolution_subtract_fusion.5
  (113 shorter events, 87.8 us)
Async XLA Ops:
  6.5 123.7 %copy-start = (f32[768,512]{1,0:T(8,128)S(1)}, f32[768,512]{1,0:T(8,128)}, u32[]{:S(2)}) copy-start(f32[768,512]{1,0:T(8,128)} %param.7) | copy-start | bytes 4718596
  6.5 123.7 %all-gather.2.cloned.1.call-start = ((), (), s32[]{:S(2)}) async-start(), calls=%async_computation | async-start | bytes 20054016 | tf_op jit(solution)/shard_map/all_gather | solution.py:22
  130.3 85.9 %all-reduce.2.cloned.1.call-start = ((), (), s32[]{:S(2)}) async-start(), calls=%async_computation.1 | async-start | bytes 3145728 | tf_op jit(solution)/shard_map/while/body/eval_jaxpr/psum | solution.py:9
  131.8 2.7 copy-start.3
  216.2 6.4 copy-start.1
  223.1 88.9 %all-reduce.2.cloned.1.call-start = ((), (), s32[]{:S(2)}) async-start(), calls=%async_computation.1 | async-start | bytes 3145728 | tf_op jit(solution)/shard_map/while/body/eval_jaxpr/psum | solution.py:9
  312.0 6.4 copy-start.1
  318.9 88.9 %all-reduce.2.cloned.1.call-start = ((), (), s32[]{:S(2)}) async-start(), calls=%async_computation.1 | async-start | bytes 3145728 | tf_op jit(solution)/shard_map/while/body/eval_jaxpr/psum | solution.py:9
  320.5 2.7 copy-start.3
  407.8 6.4 copy-start.1
  414.8 89.0 %all-reduce.2.cloned.1.call-start = ((), (), s32[]{:S(2)}) async-start(), calls=%async_computation.1 | async-start | bytes 3145728 | tf_op jit(solution)/shard_map/while/body/eval_jaxpr/psum | solution.py:9
  503.7 6.4 copy-start.1
  510.6 88.9 %all-reduce.2.cloned.1.call-start = ((), (), s32[]{:S(2)}) async-start(), calls=%async_computation.1 | async-start | bytes 3145728 | tf_op jit(solution)/shard_map/while/body/eval_jaxpr/psum | solution.py:9
  512.3 2.7 copy-start.3
  599.6 6.4 copy-start.1
  606.5 88.9 %all-reduce.2.cloned.1.call-start = ((), (), s32[]{:S(2)}) async-start(), calls=%async_computation.1 | async-start | bytes 3145728 | tf_op jit(solution)/shard_map/while/body/eval_jaxpr/psum | solution.py:9
  608.1 2.7 copy-start.3
  695.4 6.4 copy-start.1
  702.4 88.9 %all-reduce.2.cloned.1.call-start = ((), (), s32[]{:S(2)}) async-start(), calls=%async_computation.1 | async-start | bytes 3145728 | tf_op jit(solution)/shard_map/while/body/eval_jaxpr/psum | solution.py:9
  704.0 2.7 copy-start.3
  791.3 6.4 copy-start.1
  798.2 88.9 %all-reduce.2.cloned.1.call-start = ((), (), s32[]{:S(2)}) async-start(), calls=%async_computation.1 | async-start | bytes 3145728 | tf_op jit(solution)/shard_map/while/body/eval_jaxpr/psum | solution.py:9
  799.8 2.7 copy-start.3
  887.1 6.4 copy-start.1
  (3 other events, 6.5 us)
Sparse Core Ops, SparseCore 0:
  9.9 120.3 all-gather.1
  139.9 76.2 all-reduce.1
  232.7 79.1 all-reduce.1
  328.6 79.2 all-reduce.1
  424.4 79.2 all-reduce.1
  520.3 79.2 all-reduce.1
  616.2 79.2 all-reduce.1
  712.0 79.1 all-reduce.1
  807.9 79.2 all-reduce.1
where the time goes:
time: 905 us; the launch traced here: 902 us
  waiting for transfers between devices  730 us (81%)
  matrix products  116 us (13%)
  local copies, waits for them, and re-layouts  26.9 us (3%)
  other arithmetic  14.3 us (2%)
  between operations  13.1 us (1%)
    psum x8, waiting for transfers between devices, from_root(): return lax.psum(block, axis)  606 us
    all_gather x1, waiting for transfers between devices, body(): gathered = lax.all_gather(factor, 'rhs', axis=2, tiled=True)  123 us
    dot_general x48, matrix products, mult(): jnp.dot(left, right, preferred_element_type=jnp.float32, precision=lax.Pr...  116 us
    dynamic_slice x8, local copies, waits for them, and re-layouts, fetch(): return lax.dynamic_slice_in_dim(gathered, first, count, 1)  25.7 us
  transfers between devices with their start and end apart: 9, of which 9 were waited for; matrix products, arithmetic and copies ran while one was open for 3% of the time, Pallas kernels for 0%

commit v1 on v0

v1 whole, which is shorter than its diff:
```python
import functools

import jax
import jax.numpy as jnp
from jax import lax
from jax.experimental import pallas as pl
from jax.experimental.pallas import tpu as pltpu
from jax.sharding import PartitionSpec as P

MESH = pl.DeviceIdType.MESH
CHUNKS = 4
F32, BF16 = jnp.float32, jnp.bfloat16


def split(v):
    hi = v.astype(BF16)
    return hi, (v - hi.astype(F32)).astype(BF16)


def dot(a, b):
    return jnp.dot(a, b, preferred_element_type=F32)


def mult(v, wh, wl):
    hi, lo = split(v)
    m = v.shape[0]
    both = dot(jnp.concatenate([hi, lo], axis=0), wh)
    return both[:m] + (both[m:] + dot(hi, wl))


def kernel(
    n, factor, inverses, right, out,
    land, lh, ll, xb, res, sums, ih, il,
    own_sem, send_y, send_z, send_f, send_c, recv_l, recv_c,
    send_x, send_xf, recv_x, send_s, recv_s,
):
    row, rhs = lax.axis_index("row"), lax.axis_index("rhs")
    group, x = row // 4, row % 4
    yh, z, core = rhs // 8, (rhs // 2) % 4, rhs % 2
    is_a = group == 0
    is_b = group == 1
    panel = inverses.shape[1]
    block, cols = right.shape
    width = cols // n
    up_z, down_z = (z + 1) % 4, (z + 3) % 4
    right_x, left_x = (x + 1) % 4, (x + 3) % 4
    count = jnp.where(is_a, x + 5, x + 1)

    def place(group_, x_, yh_, z_, core_):
        return (group_ * 4 + x_, (yh_ * 4 + z_) * 2 + core_)

    partner = place(group, x, 1 - yh, z, core)
    above, below = place(group, x, yh, up_z, core), place(group, x, yh, down_z, core)
    twin = place(group, x, yh, z, 1 - core)
    east, west = place(group, right_x, yh, z, core), place(group, left_x, yh, z, core)
    cross = place(1 - group, x, yh, z, core)
    cross_far = place(1 - group, x, 1 - yh, z, core)

    def remote(src, dst, send, recv, device):
        return pltpu.make_async_remote_copy(
            src_ref=src, dst_ref=dst, send_sem=send, recv_sem=recv, device_id=device, device_id_type=MESH
        )

    barrier = pltpu.get_barrier_semaphore()
    for device in (partner, above, below, twin, east, west, cross, cross_far):
        pl.semaphore_signal(barrier, inc=1, device_id=device, device_id_type=MESH)
    pl.semaphore_wait(barrier, 8)

    def shard(slot, yh_, z_):
        return land.at[slot, core, :, yh_ * 4 + z_]

    def panels(index):
        return factor.at[pl.ds(3 * index, 3)]

    def send_shard(src, slot, yh_, z_, send, device):
        return remote(src, shard(slot, yh_, z_), send, recv_l.at[slot, yh_ * 4 + z_], device)

    def got_shard(slot, yh_, z_):
        send_shard(shard(slot, yh_, z_), slot, yh_, z_, send_c.at[0], partner).wait_recv()

    def own_copy(slot):
        return pltpu.make_async_copy(panels(4 * group + slot), shard(slot, yh, z), own_sem.at[slot])

    def open_own(slot, carry):
        src = panels(4 * group + slot)
        send_shard(src, slot, yh, z, send_y.at[slot, 0], partner).start()
        send_shard(src, slot, yh, z, send_z.at[slot, yh, 0], above).start()
        send_shard(src, slot, yh, z, send_z.at[slot, yh, 1], below).start()
        own_copy(slot).start()
        return carry

    def open_cross(s, carry):
        send_shard(panels(s), 4 + s, yh, z, send_y.at[4 + s, 0], cross).start()
        send_shard(panels(s), 4 + s, yh, z, send_y.at[4 + s, 1], cross_far).start()
        return carry

    lax.fori_loop(0, x + 1, open_own, 0)

    @pl.when(is_b)
    def _():
        lax.fori_loop(0, 4, open_cross, 0)

    def slot_of(v):
        return jnp.where(v <= x, v, 3 - x + v)

    def pass_on(slot, yh_):
        got_shard(slot, yh_, z)
        send_shard(shard(slot, yh_, z), slot, yh_, z, send_z.at[slot, yh_, 0], above).start()
        send_shard(shard(slot, yh_, z), slot, yh_, z, send_z.at[slot, yh_, 1], below).start()

    def far_up(slot):
        return send_shard(shard(slot, yh, down_z), slot, yh, down_z, send_f.at[slot, 0], above)

    def far_down(slot):
        return send_shard(shard(slot, 1 - yh, up_z), slot, 1 - yh, up_z, send_f.at[slot, 1], below)

    def to_twin(slot):
        return remote(land.at[slot, core], land.at[slot, core], send_c.at[slot], recv_c.at[slot], twin)

    def halves(slot):
        def piece(i, carry):
            p, yz = i // 8, i % 8
            for c in range(2):
                hi, lo = split(land[slot, c, p, yz])
                rows = hi.shape[0]
                at = pl.ds(pl.multiple_of((i * 2 + c) * rows, rows), rows)
                lh[slot, at, :] = hi
                ll[slot, at, :] = lo
            return carry

        lax.fori_loop(0, 24, piece, 0)

    def serve(v):
        def inside(u):
            return jnp.logical_and(u >= 0, u < count)

        @pl.when(inside(v + 3))
        def _():
            slot = slot_of(v + 3)
            pass_on(slot, 1 - yh)

            @pl.when(v + 3 > x)
            def _():
                pass_on(slot, yh)

        @pl.when(inside(v + 2))
        def _():
            slot = slot_of(v + 2)
            got_shard(slot, yh, down_z)
            far_up(slot).start()
            got_shard(slot, 1 - yh, up_z)
            far_down(slot).start()

        @pl.when(inside(v + 1))
        def _():
            slot = slot_of(v + 1)

            @pl.when(v + 1 <= x)
            def _():
                own_copy(slot).wait()

            got_shard(slot, 1 - yh, down_z)
            got_shard(slot, yh, up_z)
            got_shard(slot, yh, (z + 2) % 4)
            got_shard(slot, 1 - yh, (z + 2) % 4)
            to_twin(slot).start()

        @pl.when(inside(v))
        def _():
            slot = slot_of(v)
            remote(land.at[slot, 1 - core], land.at[slot, 1 - core], send_c.at[slot], recv_c.at[slot], twin).wait_recv()
            halves(slot)

    def send_own_x(c, way):
        device = (east, west)[way]
        return remote(xb.at[x, c], xb.at[x, c], send_x.at[c, way], recv_x.at[x, c], device)

    own_east = jnp.logical_or(is_a, x < 3)
    own_west = jnp.logical_or(is_a, x == 0)
    far_east = jnp.logical_or(is_a, jnp.logical_or(x == 1, x == 2))

    def forward_x(c):
        return remote(xb.at[left_x, c], xb.at[left_x, c], send_xf.at[c], recv_x.at[left_x, c], east)

    def got_x(j, c):
        remote(xb.at[j, c], xb.at[j, c], send_xf.at[c], recv_x.at[j, c], east).wait_recv()

        @pl.when(jnp.logical_and(j == left_x, far_east))
        def _():
            forward_x(c).start()

    def send_sum(c):
        return remote(sums.at[c], sums.at[c], send_s.at[c], recv_s.at[c], cross)

    def update(c, j):
        hi, lo = split(xb[j, c])
        both = jnp.concatenate([hi, lo], axis=0)
        for t in range(3):
            at = slice(t * panel, (t + 1) * panel)
            first = dot(both, lh[j, :, at])
            res[c, :, at] -= first[:width] + (first[width:] + dot(hi, ll[j, :, at]))

    def solve(c):
        @pl.when(is_b)
        def _():
            remote(sums.at[c], sums.at[c], send_s.at[c], recv_s.at[c], cross).wait_recv()
            res[c] = res[c] - sums[c]

        one, two = slice(panel, 2 * panel), slice(2 * panel, 3 * panel)
        x0 = mult(res[c, :, :panel], ih[0], il[0])
        xb[x, c, :, :panel] = x0
        rest = res[c, :, panel:] - mult(x0, lh[x, :panel, panel:], ll[x, :panel, panel:])
        x1 = mult(rest[:, :panel], ih[1], il[1])
        xb[x, c, :, one] = x1
        last = rest[:, panel:] - mult(x1, lh[x, one, two], ll[x, one, two])
        xb[x, c, :, two] = mult(last, ih[2], il[2])

        @pl.when(own_east)
        def _():
            send_own_x(c, 0).start()

        @pl.when(own_west)
        def _():
            send_own_x(c, 1).start()

        out[:, pl.ds(pl.multiple_of(c * width, width), width)] = xb[x, c].T

    for p in range(3):
        hi, lo = split(inverses[p].T)
        ih[p] = hi
        il[p] = lo

    def flip(c, carry):
        res[c] = right[:, pl.ds(pl.multiple_of(c * width, width), width)].T
        return carry

    lax.fori_loop(0, n, flip, 0)

    for v in (-3, -2, -1):
        serve(v)

    def chunk(c, carry):
        @pl.when(jnp.logical_and(c > 0, x + c < count))
        def _():
            serve(x + c)

        def earlier(j, carry):
            @pl.when(c == 0)
            def _():
                serve(j)

            @pl.when(j < x)
            def _():
                got_x(j, c)
                update(c, j)

            return carry

        lax.fori_loop(0, jnp.where(c == 0, x + 1, x), earlier, 0)
        solve(c)
        return carry

    lax.fori_loop(0, n, chunk, 0)

    @pl.when(is_a)
    def _():
        for v in range(n, 5):
            serve(x + v)

        def total(c, carry):
            def term(j, carry):
                @pl.when(j > x)
                def _():
                    got_x(j, c)

                hi, lo = split(xb[j, c])
                both = jnp.concatenate([hi, lo], axis=0)
                for t in range(3):
                    at = slice(t * panel, (t + 1) * panel)
                    first = dot(both, lh[4 + j, :, at])
                    value = first[:width] + (first[width:] + dot(hi, ll[4 + j, :, at]))
                    sums[c, :, at] = jnp.where(j == 0, 0.0, sums[c, :, at]) + value
                return carry

            lax.fori_loop(0, 4, term, 0)
            send_sum(c).start()
            return carry

        lax.fori_loop(0, n, total, 0)

    def sent_slot(v, carry):
        slot = slot_of(v)

        @pl.when(v <= x)
        def _():
            send_shard(shard(slot, yh, z), slot, yh, z, send_y.at[slot, 0], partner).wait_send()

        for a in range(2):
            for way in range(2):
                send_shard(shard(slot, yh, z), slot, yh, z, send_z.at[slot, a, way], above).wait_send()
        far_up(slot).wait_send()
        far_down(slot).wait_send()
        to_twin(slot).wait_send()
        return carry

    lax.fori_loop(0, count, sent_slot, 0)

    @pl.when(is_b)
    def _():
        def sent_cross(s, carry):
            for far in range(2):
                send_shard(panels(s), 4 + s, yh, z, send_y.at[4 + s, far], cross).wait_send()
            return carry

        lax.fori_loop(0, 4, sent_cross, 0)

    def sent_x(c, carry):
        @pl.when(own_east)
        def _():
            send_own_x(c, 0).wait_send()

        @pl.when(own_west)
        def _():
            send_own_x(c, 1).wait_send()

        @pl.when(far_east)
        def _():
            forward_x(c).wait_send()

        @pl.when(is_a)
        def _():
            send_sum(c).wait_send()

        return carry

    lax.fori_loop(0, n, sent_x, 0)


def body(factor, inverses, right_side):
    n = CHUNKS
    block, cols = right_side.shape
    panel = inverses.shape[1]
    part = factor.shape[2]
    width = cols // n
    turned = jnp.transpose(factor, (1, 2, 0))
    dma = pltpu.SemaphoreType.DMA
    vmem = pl.BlockSpec(memory_space=pltpu.VMEM)
    return pl.pallas_call(
        functools.partial(kernel, n),
        out_shape=jax.ShapeDtypeStruct((block, cols), F32),
        in_specs=[pl.BlockSpec(memory_space=pl.ANY), vmem, vmem],
        out_specs=vmem,
        scratch_shapes=[
            pltpu.VMEM((8, 2, 3, 8, part, block), F32),
            pltpu.VMEM((8, block, block), BF16),
            pltpu.VMEM((8, block, block), BF16),
            pltpu.VMEM((4, n, width, block), F32),
            pltpu.VMEM((n, width, block), F32),
            pltpu.VMEM((n, width, block), F32),
            pltpu.VMEM((3, panel, panel), BF16),
            pltpu.VMEM((3, panel, panel), BF16),
            dma((4,)),
            dma((8, 2)),
            dma((8, 2, 2)),
            dma((8, 2)),
            dma((8,)),
            dma((8, 8)),
            dma((8,)),
            dma((n, 2)),
            dma((n,)),
            dma((4, n)),
            dma((n,)),
            dma((n,)),
        ],
        compiler_params=pltpu.CompilerParams(
            collective_id=0, has_side_effects=True, vmem_limit_bytes=60 * 1024 * 1024
        ),
    )(turned, inverses, right_side)


def solution(mesh):
    placed = (P("row", None, "rhs"), P("row", None, None), P("row", "rhs"))
    return jax.shard_map(
        body, mesh=mesh, in_specs=placed, out_specs=P("row", "rhs"), check_vma=False
    )
```

time: 905 us -> 198 us (0.22)
  waiting for transfers between devices: 730 us -> 0 us
  Pallas kernels: 0 us -> 195 us
  matrix products: 116 us -> 0 us
  local copies, waits for them, and re-layouts: 26.9 us -> 2.67 us
  other arithmetic: 14.3 us -> 0 us
  between operations: 13.1 us -> 0.01 us
    psum x8 -> x0, waiting for transfers between devices: 606 us -> none  [from_root(): return lax.psum(block, axis)]
    pallas_call x0 -> x1, Pallas kernels: none -> 195 us  [body(): pl.pallas_call(functools.partial(kernel, n), out_shape=jax.ShapeDtypeStru...]
    all_gather x1 -> x0, waiting for transfers between devices: 123 us -> none  [body(): gathered = lax.all_gather(factor, 'rhs', axis=2, tiled=True)]
    dot_general x48 -> x0, matrix products: 116 us -> none  [mult(): jnp.dot(left, right, preferred_element_type=jnp.float32, precision=lax.Pr...]
    dynamic_slice x8 -> x0, local copies, waits for them, and re-layouts: 25.7 us -> none  [fetch(): return lax.dynamic_slice_in_dim(gathered, first, count, 1)]
    select_n x16 -> x0, other arithmetic: 14.3 us -> none  [the longest x8 10.5 us: from_root(): jnp.where(lax.axis_index(axis) == owner, block, jnp.zeros_like(block))]
  transfers between devices with their start and end apart: 9 -> 0, of which waited for: 9 -> 0; matrix products, arithmetic and copies ran while one was open for 3% -> 0% of each run, Pallas kernels for 0% -> 0%
where the time goes in v1:
time: 198 us; the launch traced here: 197 us
  Pallas kernels  195 us (98%)
  local copies, waits for them, and re-layouts  2.67 us (1%)
    pallas_call x1, Pallas kernels, body(): pl.pallas_call(functools.partial(kernel, n), out_shape=jax.ShapeDtypeStru...  195 us

profile of v1, /device:TPU:14, one launch (start us, length us, event | category | flops | bytes accessed | tf_op | source)
XLA Modules:
  0.0 197.4 jit_solution(7082539869286431738)
XLA Ops:
  0.0 194.7 %shard_map.37 = f32[768,512]{1,0:T(8,128)} custom-call(f32[24,16,768]{2,1,0:T(8,128)} %bitcast.1, f32[3,256,256]{2,1,0:T(8,128)} %inverses.1, f32[768,512]{1,0:T(8,128)} %right.1), custom_call_target="tpu_custom_call" | custom-call | tf_op jit(solution)/shard_map/pallas_call | solution.py:348
  194.7 2.7 %copy.5 = f32[768,512]{1,0:T(8,128)} copy(f32[768,512]{1,0:T(8,128)} %shard_map.37) | data formatting | bytes 3145728

commit v2 on v1

--- a/solution.py
+++ b/solution.py
@@ -8,7 +8,8 @@
 from jax.sharding import PartitionSpec as P
 
 MESH = pl.DeviceIdType.MESH
-CHUNKS = 4
+CHUNKS = 8
+KEPT = 2
 F32, BF16 = jnp.float32, jnp.bfloat16
 
 
@@ -31,7 +32,7 @@
 def kernel(
     n, factor, inverses, right, out,
     land, lh, ll, xb, res, sums, ih, il,
-    own_sem, send_y, send_z, send_f, send_c, recv_l, recv_c,
+    own_sem, send_y, send_b, send_z, send_f, send_c, recv_l, recv_c,
     send_x, send_xf, recv_x, send_s, recv_s,
 ):
     row, rhs = lax.axis_index("row"), lax.axis_index("rhs")
@@ -42,6 +43,7 @@
     panel = inverses.shape[1]
     block, cols = right.shape
     width = cols // n
+    per = max(1, 128 // width)
     up_z, down_z = (z + 1) % 4, (z + 3) % 4
     right_x, left_x = (x + 1) % 4, (x + 3) % 4
     count = jnp.where(is_a, x + 5, x + 1)
@@ -89,16 +91,48 @@
         own_copy(slot).start()
         return carry
 
+    def over_y(src, s, z_, far):
+        return send_shard(src, 4 + s, yh, z_, send_b.at[s, z_, far], (cross, cross_far)[far])
+
     def open_cross(s, carry):
-        send_shard(panels(s), 4 + s, yh, z, send_y.at[4 + s, 0], cross).start()
-        send_shard(panels(s), 4 + s, yh, z, send_y.at[4 + s, 1], cross_far).start()
-        return carry
-
-    lax.fori_loop(0, x + 1, open_own, 0)
+        over_y(panels(s), s, z, 0).start()
+        over_y(panels(s), s, z, 1).start()
+
+        @pl.when(s >= KEPT)
+        def _():
+            send_shard(panels(s), 4 + s, yh, z, send_z.at[4 + s, yh, 0], above).start()
+            send_shard(panels(s), 4 + s, yh, z, send_z.at[4 + s, yh, 1], below).start()
+
+        return carry
+
+    def far_cross(s, way):
+        came, to = ((down_z, above), (up_z, below))[way]
+        return send_shard(shard(4 + s, yh, came), 4 + s, yh, came, send_f.at[4 + s, 0], to)
+
+    def cross_near(s, carry):
+        for way, came in ((0, down_z), (1, up_z)):
+            got_shard(4 + s, yh, came)
+
+            @pl.when(s % 2 == way)
+            def _():
+                far_cross(s, way).start()
+
+            for far in range(2):
+                over_y(shard(4 + s, yh, came), s, came, far).start()
+        return carry
+
+    def cross_last(s, carry):
+        came = (z + 2) % 4
+        got_shard(4 + s, yh, came)
+        for far in range(2):
+            over_y(shard(4 + s, yh, came), s, came, far).start()
+        return carry
 
     @pl.when(is_b)
     def _():
         lax.fori_loop(0, 4, open_cross, 0)
+
+    lax.fori_loop(0, x + 1, open_own, 0)
 
     def slot_of(v):
         return jnp.where(v <= x, v, 3 - x + v)
@@ -134,7 +168,10 @@
         def inside(u):
             return jnp.logical_and(u >= 0, u < count)
 
-        @pl.when(inside(v + 3))
+        def relayed(u):
+            return jnp.logical_and(inside(u), u < x + 1 + KEPT)
+
+        @pl.when(relayed(v + 3))
         def _():
             slot = slot_of(v + 3)
             pass_on(slot, 1 - yh)
@@ -143,7 +180,7 @@
             def _():
                 pass_on(slot, yh)
 
-        @pl.when(inside(v + 2))
+        @pl.when(relayed(v + 2))
         def _():
             slot = slot_of(v + 2)
             got_shard(slot, yh, down_z)
@@ -159,6 +196,13 @@
             def _():
                 own_copy(slot).wait()
 
+            @pl.when(v + 1 > x + KEPT)
+            def _():
+                got_shard(slot, yh, z)
+                got_shard(slot, 1 - yh, z)
+                got_shard(slot, yh, down_z)
+                got_shard(slot, 1 - yh, up_z)
+
             got_shard(slot, 1 - yh, down_z)
             got_shard(slot, yh, up_z)
             got_shard(slot, yh, (z + 2) % 4)
@@ -176,18 +220,48 @@
         return remote(xb.at[x, c], xb.at[x, c], send_x.at[c, way], recv_x.at[x, c], device)
 
     own_east = jnp.logical_or(is_a, x < 3)
-    own_west = jnp.logical_or(is_a, x == 0)
-    far_east = jnp.logical_or(is_a, jnp.logical_or(x == 1, x == 2))
-
-    def forward_x(c):
-        return remote(xb.at[left_x, c], xb.at[left_x, c], send_xf.at[c], recv_x.at[left_x, c], east)
+
+    def own_west(c):
+        return jnp.logical_or(is_a, jnp.logical_or(x == 0, jnp.logical_and(x == 1, c % 2 == 1)))
+
+    def far_east(c):
+        low = jnp.logical_and(jnp.logical_or(x == 1, x == 2), c % 2 == 0)
+        return jnp.logical_or(low, jnp.logical_and(is_a, jnp.logical_or(x == 0, x == 3)))
+
+    def far_west(c):
+        return jnp.logical_and(jnp.logical_or(x == 0, x == 3), c % 2 == 1)
+
+    def forward_x(j, c, way):
+        return remote(xb.at[j, c], xb.at[j, c], send_xf.at[c, way], recv_x.at[j, c], (east, west)[way])
 
     def got_x(j, c):
-        remote(xb.at[j, c], xb.at[j, c], send_xf.at[c], recv_x.at[j, c], east).wait_recv()
-
-        @pl.when(jnp.logical_and(j == left_x, far_east))
-        def _():
-            forward_x(c).start()
+        remote(xb.at[j, c], xb.at[j, c], send_x.at[c, 0], recv_x.at[j, c], east).wait_recv()
+
+        @pl.when(jnp.logical_and(j == left_x, far_east(c)))
+        def _():
+            forward_x(j, c, 0).start()
+
+        @pl.when(jnp.logical_and(j == right_x, far_west(c)))
+        def _():
+            forward_x(j, c, 1).start()
+
+    def early_x(i):
+        @pl.when(jnp.logical_and(x == 3, i + 1 < n))
+        def _():
+            @pl.when(i == 0)
+            def _():
+                got_x(0, 0)
+
+            got_x(0, i + 1)
+
+        mine = jnp.logical_and(x == 0, jnp.logical_or(is_a, i % 2 == 1))
+
+        @pl.when(jnp.logical_and(mine, i >= 2))
+        def _():
+            got_x(1, i - 2)
+
+    def early(j):
+        return jnp.logical_or(jnp.logical_and(x == 3, j == 0), jnp.logical_and(x == 0, j == 1))
 
     def send_sum(c):
         return remote(sums.at[c], sums.at[c], send_s.at[c], recv_s.at[c], cross)
@@ -219,30 +293,37 @@
         def _():
             send_own_x(c, 0).start()
 
-        @pl.when(own_west)
+        @pl.when(own_west(c))
         def _():
             send_own_x(c, 1).start()
 
-        out[:, pl.ds(pl.multiple_of(c * width, width), width)] = xb[x, c].T
+        @pl.when(c % per == per - 1)
+        def _():
+            both = xb[x, pl.ds(c - (per - 1), per)].reshape(per * width, block)
+            out[:, pl.ds(pl.multiple_of((c // per) * per * width, per * width), per * width)] = both.T
 
     for p in range(3):
         hi, lo = split(inverses[p].T)
         ih[p] = hi
         il[p] = lo
 
-    def flip(c, carry):
-        res[c] = right[:, pl.ds(pl.multiple_of(c * width, width), width)].T
-        return carry
-
-    lax.fori_loop(0, n, flip, 0)
+    def flip(i, carry):
+        turned = right[:, pl.ds(pl.multiple_of(i * per * width, per * width), per * width)].T
+        res[pl.ds(i * per, per)] = turned.reshape(per, width, block)
+        return carry
+
+    lax.fori_loop(0, n // per, flip, 0)
+
+    @pl.when(is_b)
+    def _():
+        lax.fori_loop(KEPT, 4, cross_near, 0)
+        lax.fori_loop(KEPT, 4, cross_last, 0)
 
     for v in (-3, -2, -1):
         serve(v)
 
     def chunk(c, carry):
-        @pl.when(jnp.logical_and(c > 0, x + c < count))
-        def _():
-            serve(x + c)
+        early_x(c)
 
         def earlier(j, carry):
             @pl.when(c == 0)
@@ -251,7 +332,10 @@
 
             @pl.when(j < x)
             def _():
-                got_x(j, c)
+                @pl.when(jnp.logical_not(early(j)))
+                def _():
+                    got_x(j, c)
+
                 update(c, j)
 
             return carry
@@ -261,15 +345,16 @@
         return carry
 
     lax.fori_loop(0, n, chunk, 0)
+    for i in (n, n + 1):
+        early_x(i)
 
     @pl.when(is_a)
     def _():
-        for v in range(n, 5):
-            serve(x + v)
-
-        def total(c, carry):
-            def term(j, carry):
-                @pl.when(j > x)
+        def term(j, carry):
+            serve(x + 1 + j)
+
+            def total(c, carry):
+                @pl.when(jnp.logical_and(j > x, jnp.logical_not(early(j))))
                 def _():
                     got_x(j, c)
 
@@ -280,13 +365,17 @@
                     first = dot(both, lh[4 + j, :, at])
                     value = first[:width] + (first[width:] + dot(hi, ll[4 + j, :, at]))
                     sums[c, :, at] = jnp.where(j == 0, 0.0, sums[c, :, at]) + value
+
+                @pl.when(j == 3)
+                def _():
+                    send_sum(c).start()
+
                 return carry
 
-            lax.fori_loop(0, 4, term, 0)
-            send_sum(c).start()
+            lax.fori_loop(0, n, total, 0)
             return carry
 
-        lax.fori_loop(0, n, total, 0)
+        lax.fori_loop(0, 4, term, 0)
 
     def sent_slot(v, carry):
         slot = slot_of(v)
@@ -295,11 +384,14 @@
         def _():
             send_shard(shard(slot, yh, z), slot, yh, z, send_y.at[slot, 0], partner).wait_send()
 
-        for a in range(2):
-            for way in range(2):
-                send_shard(shard(slot, yh, z), slot, yh, z, send_z.at[slot, a, way], above).wait_send()
-        far_up(slot).wait_send()
-        far_down(slot).wait_send()
+        @pl.when(v < x + 1 + KEPT)
+        def _():
+            for a in range(2):
+                for way in range(2):
+                    send_shard(shard(slot, yh, z), slot, yh, z, send_z.at[slot, a, way], above).wait_send()
+            far_up(slot).wait_send()
+            far_down(slot).wait_send()
+
         to_twin(slot).wait_send()
         return carry
 
@@ -309,7 +401,17 @@
     def _():
         def sent_cross(s, carry):
             for far in range(2):
-                send_shard(panels(s), 4 + s, yh, z, send_y.at[4 + s, far], cross).wait_send()
+                over_y(panels(s), s, z, far).wait_send()
+
+            @pl.when(s >= KEPT)
+            def _():
+                for way in range(2):
+                    send_shard(panels(s), 4 + s, yh, z, send_z.at[4 + s, yh, way], above).wait_send()
+                far_cross(s, 0).wait_send()
+                for come in (up_z, down_z, (z + 2) % 4):
+                    for far in range(2):
+                        over_y(panels(s), s, come, far).wait_send()
+
             return carry
 
         lax.fori_loop(0, 4, sent_cross, 0)
@@ -319,13 +421,17 @@
         def _():
             send_own_x(c, 0).wait_send()
 
-        @pl.when(own_west)
+        @pl.when(own_west(c))
         def _():
             send_own_x(c, 1).wait_send()
 
-        @pl.when(far_east)
-        def _():
-            forward_x(c).wait_send()
+        @pl.when(far_east(c))
+        def _():
+            forward_x(x, c, 0).wait_send()
+
+        @pl.when(far_west(c))
+        def _():
+            forward_x(x, c, 1).wait_send()
 
         @pl.when(is_a)
         def _():
@@ -360,14 +466,15 @@
             pltpu.VMEM((3, panel, panel), BF16),
             pltpu.VMEM((3, panel, panel), BF16),
             dma((4,)),
-            dma((8, 2)),
+            dma((4, 1)),
+            dma((4, 4, 2)),
             dma((8, 2, 2)),
             dma((8, 2)),
             dma((8,)),
             dma((8, 8)),
             dma((8,)),
             dma((n, 2)),
-            dma((n,)),
+            dma((n, 2)),
             dma((4, n)),
             dma((n,)),
             dma((n,)),

time: 198 us -> 222 us (1.12)
  Pallas kernels: 195 us -> 219 us
    pallas_call x1, Pallas kernels: 195 us -> 219 us  [body(): pl.pallas_call(functools.partial(kernel, n), out_shape=jax.ShapeDtypeStru...]
where the time goes in v2:
time: 222 us
  Pallas kernels  219 us (99%)
  local copies, waits for them, and re-layouts  2.67 us (1%)
    pallas_call x1, Pallas kernels, body(): pl.pallas_call(functools.partial(kernel, n), out_shape=jax.ShapeDtypeStru...  219 us

profile of v2, /device:TPU:14, one launch (start us, length us, event | category | flops | bytes accessed | tf_op | source)
XLA Modules:
  0.0 221.8 jit_solution(11363714663036061566)
XLA Ops:
  0.0 219.1 %shard_map.37 = f32[768,512]{1,0:T(8,128)} custom-call(f32[24,16,768]{2,1,0:T(8,128)} %bitcast.1, f32[3,256,256]{2,1,0:T(8,128)} %inverses.1, f32[768,512]{1,0:T(8,128)} %right.1), custom_call_target="tpu_custom_call" | custom-call | tf_op jit(solution)/shard_map/pallas_call | solution.py:454
  219.1 2.7 %copy.5 = f32[768,512]{1,0:T(8,128)} copy(f32[768,512]{1,0:T(8,128)} %shard_map.37) | data formatting | bytes 3145728

commit v3 on v2

--- a/solution.py
+++ b/solution.py
@@ -9,7 +9,6 @@
 
 MESH = pl.DeviceIdType.MESH
 CHUNKS = 8
-KEPT = 2
 F32, BF16 = jnp.float32, jnp.bfloat16
 
 
@@ -46,7 +45,7 @@
     per = max(1, 128 // width)
     up_z, down_z = (z + 1) % 4, (z + 3) % 4
     right_x, left_x = (x + 1) % 4, (x + 3) % 4
-    count = jnp.where(is_a, x + 5, x + 1)
+    kept = jnp.where(x == 0, 3, jnp.where(x == 3, 1, 2))
 
     def place(group_, x_, yh_, z_, core_):
         return (group_ * 4 + x_, (yh_ * 4 + z_) * 2 + core_)
@@ -98,7 +97,7 @@
         over_y(panels(s), s, z, 0).start()
         over_y(panels(s), s, z, 1).start()
 
-        @pl.when(s >= KEPT)
+        @pl.when(s >= kept)
         def _():
             send_shard(panels(s), 4 + s, yh, z, send_z.at[4 + s, yh, 0], above).start()
             send_shard(panels(s), 4 + s, yh, z, send_z.at[4 + s, yh, 1], below).start()
@@ -133,9 +132,6 @@
         lax.fori_loop(0, 4, open_cross, 0)
 
     lax.fori_loop(0, x + 1, open_own, 0)
-
-    def slot_of(v):
-        return jnp.where(v <= x, v, 3 - x + v)
 
     def pass_on(slot, yh_):
         got_shard(slot, yh_, z)
@@ -164,56 +160,43 @@
 
         lax.fori_loop(0, 24, piece, 0)
 
-    def serve(v):
-        def inside(u):
-            return jnp.logical_and(u >= 0, u < count)
-
-        def relayed(u):
-            return jnp.logical_and(inside(u), u < x + 1 + KEPT)
-
-        @pl.when(relayed(v + 3))
-        def _():
-            slot = slot_of(v + 3)
-            pass_on(slot, 1 - yh)
-
-            @pl.when(v + 3 > x)
-            def _():
-                pass_on(slot, yh)
-
-        @pl.when(relayed(v + 2))
-        def _():
-            slot = slot_of(v + 2)
-            got_shard(slot, yh, down_z)
-            far_up(slot).start()
-            got_shard(slot, 1 - yh, up_z)
-            far_down(slot).start()
-
-        @pl.when(inside(v + 1))
-        def _():
-            slot = slot_of(v + 1)
-
-            @pl.when(v + 1 <= x)
-            def _():
-                own_copy(slot).wait()
-
-            @pl.when(v + 1 > x + KEPT)
-            def _():
-                got_shard(slot, yh, z)
-                got_shard(slot, 1 - yh, z)
-                got_shard(slot, yh, down_z)
-                got_shard(slot, 1 - yh, up_z)
-
-            got_shard(slot, 1 - yh, down_z)
-            got_shard(slot, yh, up_z)
-            got_shard(slot, yh, (z + 2) % 4)
-            got_shard(slot, 1 - yh, (z + 2) % 4)
-            to_twin(slot).start()
-
-        @pl.when(inside(v))
-        def _():
-            slot = slot_of(v)
-            remote(land.at[slot, 1 - core], land.at[slot, 1 - core], send_c.at[slot], recv_c.at[slot], twin).wait_recv()
-            halves(slot)
+    def far_on(slot):
+        got_shard(slot, yh, down_z)
+        far_up(slot).start()
+        got_shard(slot, 1 - yh, up_z)
+        far_down(slot).start()
+
+    def far_here(slot):
+        got_shard(slot, 1 - yh, down_z)
+        got_shard(slot, yh, up_z)
+        got_shard(slot, yh, (z + 2) % 4)
+        got_shard(slot, 1 - yh, (z + 2) % 4)
+
+    def finish(slot):
+        remote(land.at[slot, 1 - core], land.at[slot, 1 - core], send_c.at[slot], recv_c.at[slot], twin).wait_recv()
+        halves(slot)
+
+    def pass_on_cross(s, carry):
+        pass_on(4 + s, 0)
+        pass_on(4 + s, 1)
+        return carry
+
+    def close_cross(s, carry):
+        @pl.when(s >= kept)
+        def _():
+            got_shard(4 + s, yh, z)
+            got_shard(4 + s, 1 - yh, z)
+            got_shard(4 + s, yh, down_z)
+            got_shard(4 + s, 1 - yh, up_z)
+
+        far_here(4 + s)
+        to_twin(4 + s).start()
+
+        @pl.when(s > 0)
+        def _():
+            finish(3 + s)
+
+        return carry
 
     def send_own_x(c, way):
         device = (east, west)[way]
@@ -225,11 +208,15 @@
         return jnp.logical_or(is_a, jnp.logical_or(x == 0, jnp.logical_and(x == 1, c % 2 == 1)))
 
     def far_east(c):
-        low = jnp.logical_and(jnp.logical_or(x == 1, x == 2), c % 2 == 0)
-        return jnp.logical_or(low, jnp.logical_and(is_a, jnp.logical_or(x == 0, x == 3)))
+        on_a = jnp.logical_or(x == 0, jnp.logical_and(x == 2, c < 2))
+        on_b = jnp.logical_and(x == 2, c % 2 == 0)
+        return jnp.logical_or(jnp.logical_and(is_a, on_a), jnp.logical_and(is_b, on_b))
 
     def far_west(c):
-        return jnp.logical_and(jnp.logical_or(x == 0, x == 3), c % 2 == 1)
+        on_a = jnp.logical_or(x == 1, jnp.logical_and(x == 0, c >= 2))
+        on_b = jnp.logical_and(x == 0, c % 2 == 1)
+        either = jnp.logical_or(jnp.logical_and(is_a, on_a), jnp.logical_and(is_b, on_b))
+        return jnp.logical_or(x == 3, either)
 
     def forward_x(j, c, way):
         return remote(xb.at[j, c], xb.at[j, c], send_xf.at[c, way], recv_x.at[j, c], (east, west)[way])
@@ -245,8 +232,20 @@
         def _():
             forward_x(j, c, 1).start()
 
+    step = n // 4
+
+    def early_group(v):
+        @pl.when(jnp.logical_and(is_a, x == 3))
+        def _():
+            for k in range(step):
+                got_x(0, v * step + k)
+
+        @pl.when(jnp.logical_and(jnp.logical_and(is_a, x == 2), v >= 1))
+        def _():
+            got_x(1, v - 1)
+
     def early_x(i):
-        @pl.when(jnp.logical_and(x == 3, i + 1 < n))
+        @pl.when(jnp.logical_and(jnp.logical_and(is_b, x == 3), i + 1 < n))
         def _():
             @pl.when(i == 0)
             def _():
@@ -254,14 +253,17 @@
 
             got_x(0, i + 1)
 
-        mine = jnp.logical_and(x == 0, jnp.logical_or(is_a, i % 2 == 1))
-
-        @pl.when(jnp.logical_and(mine, i >= 2))
-        def _():
-            got_x(1, i - 2)
-
-    def early(j):
-        return jnp.logical_or(jnp.logical_and(x == 3, j == 0), jnp.logical_and(x == 0, j == 1))
+        @pl.when(jnp.logical_and(jnp.logical_and(is_b, x == 0), jnp.logical_and(i >= 3, i % 2 == 0)))
+        def _():
+            got_x(1, i - 3)
+
+        @pl.when(jnp.logical_and(jnp.logical_and(is_a, x == 1), i >= n - 2))
+        def _():
+            got_x(2, i - (n - 2))
+
+    def early(j, c):
+        second = jnp.logical_and(jnp.logical_and(is_a, x == 2), jnp.logical_and(j == 1, c < 2))
+        return jnp.logical_or(jnp.logical_and(x == 3, j == 0), second)
 
     def send_sum(c):
         return remote(sums.at[c], sums.at[c], send_s.at[c], recv_s.at[c], cross)
@@ -316,86 +318,147 @@
 
     @pl.when(is_b)
     def _():
-        lax.fori_loop(KEPT, 4, cross_near, 0)
-        lax.fori_loop(KEPT, 4, cross_last, 0)
-
-    for v in (-3, -2, -1):
-        serve(v)
-
-    def chunk(c, carry):
+        lax.fori_loop(kept, 4, cross_near, 0)
+        lax.fori_loop(kept, 4, cross_last, 0)
+
+    def own_group(v, carry):
+        @pl.when(v + 2 <= x)
+        def _():
+            pass_on(v + 2, 1 - yh)
+
+        @pl.when(v + 1 <= x)
+        def _():
+            far_on(v + 1)
+
+        return carry
+
+    pass_on(0, 1 - yh)
+
+    @pl.when(x >= 1)
+    def _():
+        pass_on(1, 1 - yh)
+
+    far_on(0)
+
+    def one_chunk(c, first):
         early_x(c)
 
         def earlier(j, carry):
-            @pl.when(c == 0)
-            def _():
-                serve(j)
+            if first:
+                own_copy(j).wait()
+                far_here(j)
+                to_twin(j).start()
+                finish(j)
+                early_group(j)
 
             @pl.when(j < x)
             def _():
-                @pl.when(jnp.logical_not(early(j)))
+                @pl.when(jnp.logical_not(early(j, c)))
                 def _():
                     got_x(j, c)
 
                 update(c, j)
 
+            if first:
+                own_group(j, 0)
+
+                @pl.when(jnp.logical_and(is_a, j == x - 1))
+                def _():
+                    lax.fori_loop(0, kept, pass_on_cross, 0)
+
             return carry
 
-        lax.fori_loop(0, jnp.where(c == 0, x + 1, x), earlier, 0)
+        lax.fori_loop(0, x + 1 if first else x, earlier, 0)
         solve(c)
-        return carry
-
-    lax.fori_loop(0, n, chunk, 0)
-    for i in (n, n + 1):
-        early_x(i)
+
+        @pl.when(jnp.logical_and(jnp.logical_and(is_a, x > 0), jnp.logical_and(c % 2 == 1, c // 2 < kept)))
+        def _():
+            far_on(4 + c // 2)
+
+    def chunk(c, carry):
+        one_chunk(c, False)
+        return carry
+
+    one_chunk(0, True)
+    lax.fori_loop(1, n, chunk, 0)
+    for i in range(n, n + 3):
+
+        @pl.when(is_b)
+        def _():
+            early_x(i)
 
     @pl.when(is_a)
     def _():
-        def term(j, carry):
-            serve(x + 1 + j)
-
-            def total(c, carry):
-                @pl.when(jnp.logical_and(j > x, jnp.logical_not(early(j))))
-                def _():
-                    got_x(j, c)
-
-                hi, lo = split(xb[j, c])
-                both = jnp.concatenate([hi, lo], axis=0)
-                for t in range(3):
-                    at = slice(t * panel, (t + 1) * panel)
-                    first = dot(both, lh[4 + j, :, at])
-                    value = first[:width] + (first[width:] + dot(hi, ll[4 + j, :, at]))
-                    sums[c, :, at] = jnp.where(j == 0, 0.0, sums[c, :, at]) + value
-
-                @pl.when(j == 3)
-                def _():
-                    send_sum(c).start()
-
+        @pl.when(x == 0)
+        def _():
+            def far_cross_group(s, carry):
+                far_on(4 + s)
                 return carry
 
-            lax.fori_loop(0, n, total, 0)
+            lax.fori_loop(0, kept, pass_on_cross, 0)
+            lax.fori_loop(0, kept, far_cross_group, 0)
+
+        lax.fori_loop(0, 4, close_cross, 0)
+        finish(7)
+        ahead = jnp.where(x == 1, 2, 0)
+        behind = jnp.where(x == 0, n // 2, 0)
+
+        def total(i, carry):
+            @pl.when(jnp.logical_and(x < 2, i + ahead < n))
+            def _():
+                got_x(x + 1, i + ahead)
+
+            c = i - behind
+
+            @pl.when(jnp.logical_and(c >= 0, c < n))
+            def _():
+                def term(j, carry):
+                    @pl.when(jnp.logical_and(j > x, jnp.logical_or(x >= 2, j > x + 1)))
+                    def _():
+                        got_x(j, c)
+
+                    hi, lo = split(xb[j, c])
+                    both = jnp.concatenate([hi, lo], axis=0)
+                    for t in range(3):
+                        at = slice(t * panel, (t + 1) * panel)
+                        first = dot(both, lh[4 + j, :, at])
+                        value = first[:width] + (first[width:] + dot(hi, ll[4 + j, :, at]))
+                        sums[c, :, at] = jnp.where(j == 0, 0.0, sums[c, :, at]) + value
+                    return carry
+
+                lax.fori_loop(0, 4, term, 0)
+                send_sum(c).start()
+
             return carry
 
-        lax.fori_loop(0, 4, term, 0)
-
-    def sent_slot(v, carry):
-        slot = slot_of(v)
-
-        @pl.when(v <= x)
-        def _():
-            send_shard(shard(slot, yh, z), slot, yh, z, send_y.at[slot, 0], partner).wait_send()
-
-        @pl.when(v < x + 1 + KEPT)
-        def _():
-            for a in range(2):
-                for way in range(2):
-                    send_shard(shard(slot, yh, z), slot, yh, z, send_z.at[slot, a, way], above).wait_send()
-            far_up(slot).wait_send()
-            far_down(slot).wait_send()
-
+        lax.fori_loop(0, n + behind, total, 0)
+
+    def sent_ring(slot):
+        for a in range(2):
+            for way in range(2):
+                send_shard(shard(slot, yh, z), slot, yh, z, send_z.at[slot, a, way], above).wait_send()
+        far_up(slot).wait_send()
+        far_down(slot).wait_send()
+
+    def sent_own(slot, carry):
+        send_shard(shard(slot, yh, z), slot, yh, z, send_y.at[slot, 0], partner).wait_send()
+        sent_ring(slot)
         to_twin(slot).wait_send()
         return carry
 
-    lax.fori_loop(0, count, sent_slot, 0)
+    lax.fori_loop(0, x + 1, sent_own, 0)
+
+    @pl.when(is_a)
+    def _():
+        def sent_used(s, carry):
+            @pl.when(s < kept)
+            def _():
+                sent_ring(4 + s)
+
+            to_twin(4 + s).wait_send()
+            return carry
+
+        lax.fori_loop(0, 4, sent_used, 0)
 
     @pl.when(is_b)
     def _():
@@ -403,7 +466,7 @@
             for far in range(2):
                 over_y(panels(s), s, z, far).wait_send()
 
-            @pl.when(s >= KEPT)
+            @pl.when(s >= kept)
             def _():
                 for way in range(2):
                     send_shard(panels(s), 4 + s, yh, z, send_z.at[4 + s, yh, way], above).wait_send()

time: 222 us -> 202 us (0.910)
  Pallas kernels: 219 us -> 199 us
    pallas_call x1, Pallas kernels: 219 us -> 199 us  [body(): pl.pallas_call(functools.partial(kernel, n), out_shape=jax.ShapeDtypeStru...]
where the time goes in v3:
time: 202 us; the launch traced here: 201 us
  Pallas kernels  199 us (99%)
  local copies, waits for them, and re-layouts  2.67 us (1%)
    pallas_call x1, Pallas kernels, body(): pl.pallas_call(functools.partial(kernel, n), out_shape=jax.ShapeDtypeStru...  199 us

profile of v3, /device:TPU:14, one launch (start us, length us, event | category | flops | bytes accessed | tf_op | source)
XLA Modules:
  0.0 201.5 jit_solution(16216374033530760364)
XLA Ops:
  0.0 198.8 %shard_map.37 = f32[768,512]{1,0:T(8,128)} custom-call(f32[24,16,768]{2,1,0:T(8,128)} %bitcast.1, f32[3,256,256]{2,1,0:T(8,128)} %inverses.1, f32[768,512]{1,0:T(8,128)} %right.1), custom_call_target="tpu_custom_call" | custom-call | tf_op jit(solution)/shard_map/pallas_call | solution.py:517
  198.8 2.7 %copy.5 = f32[768,512]{1,0:T(8,128)} copy(f32[768,512]{1,0:T(8,128)} %shard_map.37) | data formatting | bytes 3145728

commit v4 on v3

--- a/solution.py
+++ b/solution.py
@@ -9,6 +9,9 @@
 
 MESH = pl.DeviceIdType.MESH
 CHUNKS = 8
+LEAD = 3
+BEHIND2 = 4
+BEHIND3 = 2
 F32, BF16 = jnp.float32, jnp.bfloat16
 
 
@@ -62,33 +65,76 @@
             src_ref=src, dst_ref=dst, send_sem=send, recv_sem=recv, device_id=device, device_id_type=MESH
         )
 
+    def shard(slot, yh_, z_, k=3):
+        return land.at[slot, core, pl.ds(0, k), yh_ * 4 + z_]
+
+    def panels(index):
+        return factor.at[pl.ds(3 * index, 3)]
+
+    def send_shard(src, slot, yh_, z_, send, device, k=3):
+        return remote(src, shard(slot, yh_, z_, k), send, recv_l.at[slot, yh_ * 4 + z_], device)
+
+    def got_shard(slot, yh_, z_, k=3):
+        send_shard(shard(slot, yh_, z_, k), slot, yh_, z_, send_c.at[0], partner, k).wait_recv()
+
+    def relay(slot, yh_, z_, send, device, k=3):
+        return send_shard(shard(slot, yh_, z_, k), slot, yh_, z_, send, device, k)
+
+    def own_copy(slot):
+        return pltpu.make_async_copy(panels(4 * group + slot), shard(slot, yh, z), own_sem.at[slot])
+
+    def corner(k):
+        first = 3 * (4 * group + x)
+        here = land.at[x, core, 0, yh * 4 + z]
+        if k == 0:
+            src, dst = factor.at[first, :, pl.ds(panel, 2 * panel)], here.at[:, pl.ds(panel, 2 * panel)]
+        else:
+            src, dst = factor.at[first + 1, :, pl.ds(2 * panel, panel)], here.at[:, pl.ds(0, panel)]
+        return pltpu.make_async_copy(src, dst, own_sem.at[4 + k])
+
+    def open_own(slot, carry):
+        src = panels(4 * group + slot)
+        send_shard(src, slot, yh, z, send_y.at[slot, z], partner).start()
+        send_shard(src, slot, yh, z, send_z.at[slot, yh, 0], above).start()
+        send_shard(src, slot, yh, z, send_z.at[slot, yh, 1], below).start()
+        own_copy(slot).start()
+        return carry
+
+    def open_corner():
+        corner(0).wait()
+        corner(1).wait()
+        relay(x, yh, z, send_y.at[x, z], partner, 1).start()
+        relay(x, yh, z, send_z.at[x, yh, 0], above, 1).start()
+        relay(x, yh, z, send_z.at[x, yh, 1], below, 1).start()
+
+    def along_first(slot):
+        return jnp.logical_and(jnp.logical_and(slot >= 1, slot <= 2), slot < x)
+
+    def ring_one(slot, way):
+        came, to = ((down_z, above), (up_z, below))[way]
+        return relay(slot, yh, came, send_f.at[slot, 0], to)
+
+    def along_near(slot):
+        for way, came in ((0, down_z), (1, up_z)):
+            got_shard(slot, yh, came)
+
+            @pl.when(slot % 2 == way)
+            def _():
+                ring_one(slot, way).start()
+
+            relay(slot, yh, came, send_y.at[slot, came], partner).start()
+
+    def along_last(slot):
+        came = (z + 2) % 4
+        got_shard(slot, yh, came)
+        relay(slot, yh, came, send_y.at[slot, came], partner).start()
+
+    corner(0).start()
+    corner(1).start()
     barrier = pltpu.get_barrier_semaphore()
     for device in (partner, above, below, twin, east, west, cross, cross_far):
         pl.semaphore_signal(barrier, inc=1, device_id=device, device_id_type=MESH)
     pl.semaphore_wait(barrier, 8)
-
-    def shard(slot, yh_, z_):
-        return land.at[slot, core, :, yh_ * 4 + z_]
-
-    def panels(index):
-        return factor.at[pl.ds(3 * index, 3)]
-
-    def send_shard(src, slot, yh_, z_, send, device):
-        return remote(src, shard(slot, yh_, z_), send, recv_l.at[slot, yh_ * 4 + z_], device)
-
-    def got_shard(slot, yh_, z_):
-        send_shard(shard(slot, yh_, z_), slot, yh_, z_, send_c.at[0], partner).wait_recv()
-
-    def own_copy(slot):
-        return pltpu.make_async_copy(panels(4 * group + slot), shard(slot, yh, z), own_sem.at[slot])
-
-    def open_own(slot, carry):
-        src = panels(4 * group + slot)
-        send_shard(src, slot, yh, z, send_y.at[slot, 0], partner).start()
-        send_shard(src, slot, yh, z, send_z.at[slot, yh, 0], above).start()
-        send_shard(src, slot, yh, z, send_z.at[slot, yh, 1], below).start()
-        own_copy(slot).start()
-        return carry
 
     def over_y(src, s, z_, far):
         return send_shard(src, 4 + s, yh, z_, send_b.at[s, z_, far], (cross, cross_far)[far])
@@ -131,23 +177,25 @@
     def _():
         lax.fori_loop(0, 4, open_cross, 0)
 
-    lax.fori_loop(0, x + 1, open_own, 0)
-
-    def pass_on(slot, yh_):
-        got_shard(slot, yh_, z)
-        send_shard(shard(slot, yh_, z), slot, yh_, z, send_z.at[slot, yh_, 0], above).start()
-        send_shard(shard(slot, yh_, z), slot, yh_, z, send_z.at[slot, yh_, 1], below).start()
-
-    def far_up(slot):
-        return send_shard(shard(slot, yh, down_z), slot, yh, down_z, send_f.at[slot, 0], above)
-
-    def far_down(slot):
-        return send_shard(shard(slot, 1 - yh, up_z), slot, 1 - yh, up_z, send_f.at[slot, 1], below)
-
-    def to_twin(slot):
-        return remote(land.at[slot, core], land.at[slot, core], send_c.at[slot], recv_c.at[slot], twin)
-
-    def halves(slot):
+    lax.fori_loop(0, x, open_own, 0)
+    open_corner()
+
+    def pass_on(slot, yh_, k=3):
+        got_shard(slot, yh_, z, k)
+        relay(slot, yh_, z, send_z.at[slot, yh_, 0], above, k).start()
+        relay(slot, yh_, z, send_z.at[slot, yh_, 1], below, k).start()
+
+    def far_up(slot, k=3):
+        return relay(slot, yh, down_z, send_f.at[slot, 0], above, k)
+
+    def far_down(slot, k=3):
+        return relay(slot, 1 - yh, up_z, send_f.at[slot, 1], below, k)
+
+    def to_twin(slot, k=3):
+        part = land.at[slot, core, pl.ds(0, k)]
+        return remote(part, part, send_c.at[slot], recv_c.at[slot], twin)
+
+    def halves(slot, k=3):
         def piece(i, carry):
             p, yz = i // 8, i % 8
             for c in range(2):
@@ -158,23 +206,24 @@
                 ll[slot, at, :] = lo
             return carry
 
-        lax.fori_loop(0, 24, piece, 0)
-
-    def far_on(slot):
-        got_shard(slot, yh, down_z)
-        far_up(slot).start()
-        got_shard(slot, 1 - yh, up_z)
-        far_down(slot).start()
-
-    def far_here(slot):
-        got_shard(slot, 1 - yh, down_z)
-        got_shard(slot, yh, up_z)
-        got_shard(slot, yh, (z + 2) % 4)
-        got_shard(slot, 1 - yh, (z + 2) % 4)
-
-    def finish(slot):
-        remote(land.at[slot, 1 - core], land.at[slot, 1 - core], send_c.at[slot], recv_c.at[slot], twin).wait_recv()
-        halves(slot)
+        lax.fori_loop(0, 8 * k, piece, 0)
+
+    def far_on(slot, k=3):
+        got_shard(slot, yh, down_z, k)
+        far_up(slot, k).start()
+        got_shard(slot, 1 - yh, up_z, k)
+        far_down(slot, k).start()
+
+    def far_here(slot, k=3):
+        got_shard(slot, 1 - yh, down_z, k)
+        got_shard(slot, yh, up_z, k)
+        got_shard(slot, yh, (z + 2) % 4, k)
+        got_shard(slot, 1 - yh, (z + 2) % 4, k)
+
+    def finish(slot, k=3):
+        part = land.at[slot, 1 - core, pl.ds(0, k)]
+        remote(part, part, send_c.at[slot], recv_c.at[slot], twin).wait_recv()
+        halves(slot, k)
 
     def pass_on_cross(s, carry):
         pass_on(4 + s, 0)
@@ -182,6 +231,11 @@
         return carry
 
     def close_cross(s, carry):
+        @pl.when(x == 0)
+        def _():
+            for k in range(n // 8):
+                got_x(1, n // 2 + s * (n // 8) + k)
+
         @pl.when(s >= kept)
         def _():
             got_shard(4 + s, yh, z)
@@ -240,18 +294,15 @@
             for k in range(step):
                 got_x(0, v * step + k)
 
-        @pl.when(jnp.logical_and(jnp.logical_and(is_a, x == 2), v >= 1))
-        def _():
-            got_x(1, v - 1)
-
     def early_x(i):
-        @pl.when(jnp.logical_and(jnp.logical_and(is_b, x == 3), i + 1 < n))
+        @pl.when(jnp.logical_and(jnp.logical_and(is_b, x == 3), i + LEAD < n))
         def _():
             @pl.when(i == 0)
             def _():
-                got_x(0, 0)
-
-            got_x(0, i + 1)
+                for k in range(LEAD):
+                    got_x(0, k)
+
+            got_x(0, i + LEAD)
 
         @pl.when(jnp.logical_and(jnp.logical_and(is_b, x == 0), jnp.logical_and(i >= 3, i % 2 == 0)))
         def _():
@@ -261,9 +312,8 @@
         def _():
             got_x(2, i - (n - 2))
 
-    def early(j, c):
-        second = jnp.logical_and(jnp.logical_and(is_a, x == 2), jnp.logical_and(j == 1, c < 2))
-        return jnp.logical_or(jnp.logical_and(x == 3, j == 0), second)
+    def early(j):
+        return jnp.logical_and(x == 3, j == 0)
 
     def send_sum(c):
         return remote(sums.at[c], sums.at[c], send_s.at[c], recv_s.at[c], cross)
@@ -288,7 +338,7 @@
         rest = res[c, :, panel:] - mult(x0, lh[x, :panel, panel:], ll[x, :panel, panel:])
         x1 = mult(rest[:, :panel], ih[1], il[1])
         xb[x, c, :, one] = x1
-        last = rest[:, panel:] - mult(x1, lh[x, one, two], ll[x, one, two])
+        last = rest[:, panel:] - mult(x1, lh[x, :panel, :panel], ll[x, :panel, :panel])
         xb[x, c, :, two] = mult(last, ih[2], il[2])
 
         @pl.when(own_east)
@@ -321,66 +371,128 @@
         lax.fori_loop(kept, 4, cross_near, 0)
         lax.fori_loop(kept, 4, cross_last, 0)
 
+    def by_kind(slot, on_corner, on_along, on_plain):
+        @pl.when(slot == x)
+        def _():
+            on_corner()
+
+        @pl.when(slot < x)
+        def _():
+            along = along_first(slot)
+
+            @pl.when(along)
+            def _():
+                on_along()
+
+            @pl.when(jnp.logical_not(along))
+            def _():
+                on_plain()
+
+    def own_near(u):
+        by_kind(u, lambda: pass_on(u, 1 - yh, 1), lambda: along_near(u), lambda: pass_on(u, 1 - yh))
+
+    def own_far(u):
+        by_kind(u, lambda: far_on(u, 1), lambda: along_last(u), lambda: far_on(u))
+
+    def own_all(u):
+        def corner_all():
+            far_here(u, 1)
+            to_twin(u, 1).start()
+
+        def along_all():
+            own_copy(u).wait()
+            for z_ in range(4):
+                got_shard(u, 1 - yh, z_)
+            to_twin(u).start()
+
+        def plain_all():
+            own_copy(u).wait()
+            far_here(u)
+            to_twin(u).start()
+
+        by_kind(u, corner_all, along_all, plain_all)
+
     def own_group(v, carry):
-        @pl.when(v + 2 <= x)
-        def _():
-            pass_on(v + 2, 1 - yh)
-
-        @pl.when(v + 1 <= x)
-        def _():
-            far_on(v + 1)
-
-        return carry
-
-    pass_on(0, 1 - yh)
-
-    @pl.when(x >= 1)
-    def _():
-        pass_on(1, 1 - yh)
-
-    far_on(0)
-
-    def one_chunk(c, first):
+        own_all(v)
+        own_near(v + 2)
+        own_far(v + 1)
+
+        @pl.when(jnp.logical_and(is_a, v == x - 1))
+        def _():
+            lax.fori_loop(0, kept, pass_on_cross, 0)
+
+        by_kind(v, lambda: finish(v, 1), lambda: finish(v), lambda: finish(v))
+        early_group(v)
+        return carry
+
+    own_near(0)
+    own_near(1)
+    own_far(0)
+    lax.fori_loop(0, x + 1, own_group, 0)
+
+    ahead = jnp.where(x == 1, 2, 0)
+    behind = jnp.where(x == 3, BEHIND3, jnp.where(x == 2, BEHIND2, n))
+
+    def total(c, carry):
+        @pl.when(jnp.logical_and(x == 1, c + ahead < n))
+        def _():
+            got_x(x + 1, c + ahead)
+
+        def term(j, carry):
+            @pl.when(jnp.logical_and(j > x, jnp.logical_or(x >= 2, j > x + 1)))
+            def _():
+                got_x(j, c)
+
+            hi, lo = split(xb[j, c])
+            both = jnp.concatenate([hi, lo], axis=0)
+            for t in range(3):
+                at = slice(t * panel, (t + 1) * panel)
+                first = dot(both, lh[4 + j, :, at])
+                value = first[:width] + (first[width:] + dot(hi, ll[4 + j, :, at]))
+                sums[c, :, at] = jnp.where(j == 0, 0.0, sums[c, :, at]) + value
+            return carry
+
+        lax.fori_loop(0, 4, term, 0)
+        send_sum(c).start()
+
+        return carry
+
+    def close_all():
+        lax.fori_loop(0, 4, close_cross, 0)
+        finish(7)
+
+    def chunk(c, carry):
         early_x(c)
 
         def earlier(j, carry):
-            if first:
-                own_copy(j).wait()
-                far_here(j)
-                to_twin(j).start()
-                finish(j)
-                early_group(j)
-
             @pl.when(j < x)
             def _():
-                @pl.when(jnp.logical_not(early(j, c)))
+                @pl.when(jnp.logical_not(early(j)))
                 def _():
                     got_x(j, c)
 
                 update(c, j)
 
-            if first:
-                own_group(j, 0)
-
-                @pl.when(jnp.logical_and(is_a, j == x - 1))
-                def _():
-                    lax.fori_loop(0, kept, pass_on_cross, 0)
-
             return carry
 
-        lax.fori_loop(0, x + 1 if first else x, earlier, 0)
+        lax.fori_loop(0, x, earlier, 0)
         solve(c)
 
         @pl.when(jnp.logical_and(jnp.logical_and(is_a, x > 0), jnp.logical_and(c % 2 == 1, c // 2 < kept)))
         def _():
             far_on(4 + c // 2)
 
-    def chunk(c, carry):
-        one_chunk(c, False)
-        return carry
-
-    one_chunk(0, True)
-    lax.fori_loop(1, n, chunk, 0)
+        @pl.when(jnp.logical_and(is_a, c >= behind))
+        def _():
+            @pl.when(c == behind)
+            def _():
+                close_all()
+
+            total(c - behind, 0)
+
+        return carry
+
+    lax.fori_loop(0, n, chunk, 0)
     for i in range(n, n + 3):
 
         @pl.when(is_b)
@@ -391,59 +503,52 @@
     def _():
         @pl.when(x == 0)
         def _():
+            def pass_second(c, carry):
+                got_x(1, c)
+                return carry
+
             def far_cross_group(s, carry):
                 far_on(4 + s)
                 return carry
 
             lax.fori_loop(0, kept, pass_on_cross, 0)
-            lax.fori_loop(0, kept, far_cross_group, 0)
-
-        lax.fori_loop(0, 4, close_cross, 0)
-        finish(7)
-        ahead = jnp.where(x == 1, 2, 0)
-        behind = jnp.where(x == 0, n // 2, 0)
-
-        def total(i, carry):
-            @pl.when(jnp.logical_and(x < 2, i + ahead < n))
-            def _():
-                got_x(x + 1, i + ahead)
-
-            c = i - behind
-
-            @pl.when(jnp.logical_and(c >= 0, c < n))
-            def _():
-                def term(j, carry):
-                    @pl.when(jnp.logical_and(j > x, jnp.logical_or(x >= 2, j > x + 1)))
-                    def _():
-                        got_x(j, c)
-
-                    hi, lo = split(xb[j, c])
-                    both = jnp.concatenate([hi, lo], axis=0)
-                    for t in range(3):
-                        at = slice(t * panel, (t + 1) * panel)
-                        first = dot(both, lh[4 + j, :, at])
-                        value = first[:width] + (first[width:] + dot(hi, ll[4 + j, :, at]))
-                        sums[c, :, at] = jnp.where(j == 0, 0.0, sums[c, :, at]) + value
-                    return carry
-
-                lax.fori_loop(0, 4, term, 0)
-                send_sum(c).start()
-
-            return carry
-
-        lax.fori_loop(0, n + behind, total, 0)
-
-    def sent_ring(slot):
+            lax.fori_loop(0, kept - 1, far_cross_group, 0)
+            lax.fori_loop(0, n // 2, pass_second, 0)
+            lax.fori_loop(kept - 1, kept, far_cross_group, 0)
+
+        @pl.when(x < 2)
+        def _():
+            close_all()
+
+        lax.fori_loop(n - behind, n, total, 0)
+
+    def sent_ring(slot, k=3):
         for a in range(2):
             for way in range(2):
-                send_shard(shard(slot, yh, z), slot, yh, z, send_z.at[slot, a, way], above).wait_send()
-        far_up(slot).wait_send()
-        far_down(slot).wait_send()
+                relay(slot, yh, z, send_z.at[slot, a, way], above, k).wait_send()
+        far_up(slot, k).wait_send()
+        far_down(slot, k).wait_send()
 
     def sent_own(slot, carry):
-        send_shard(shard(slot, yh, z), slot, yh, z, send_y.at[slot, 0], partner).wait_send()
-        sent_ring(slot)
-        to_twin(slot).wait_send()
+        def corner_sent():
+            relay(slot, yh, z, send_y.at[slot, z], partner, 1).wait_send()
+            sent_ring(slot, 1)
+            to_twin(slot, 1).wait_send()
+
+        def along_sent():
+            for z_ in range(4):
+                relay(slot, yh, z, send_y.at[slot, z_], partner).wait_send()
+            for way in range(2):
+                relay(slot, yh, z, send_z.at[slot, yh, way], above).wait_send()
+            ring_one(slot, 0).wait_send()
+            to_twin(slot).wait_send()
+
+        def plain_sent():
+            relay(slot, yh, z, send_y.at[slot, z], partner).wait_send()
+            sent_ring(slot)
+            to_twin(slot).wait_send()
+
+        by_kind(slot, corner_sent, along_sent, plain_sent)
         return carry
 
     lax.fori_loop(0, x + 1, sent_own, 0)
@@ -528,8 +633,8 @@
             pltpu.VMEM((n, width, block), F32),
             pltpu.VMEM((3, panel, panel), BF16),
             pltpu.VMEM((3, panel, panel), BF16),
-            dma((4,)),
-            dma((4, 1)),
+            dma((6,)),
+            dma((4, 4)),
             dma((4, 4, 2)),
             dma((8, 2, 2)),
             dma((8, 2)),

time: 202 us -> 156 us (0.77)
  Pallas kernels: 199 us -> 153 us
    pallas_call x1, Pallas kernels: 199 us -> 153 us  [body(): pl.pallas_call(functools.partial(kernel, n), out_shape=jax.ShapeDtypeStru...]
where the time goes in v4:
time: 156 us
  Pallas kernels  153 us (98%)
  local copies, waits for them, and re-layouts  2.67 us (2%)
    pallas_call x1, Pallas kernels, body(): pl.pallas_call(functools.partial(kernel, n), out_shape=jax.ShapeDtypeStru...  153 us

profile of v4, /device:TPU:14, one launch (start us, length us, event | category | flops | bytes accessed | tf_op | source)
XLA Modules:
  0.0 156.1 jit_solution(17553489321763232377)
XLA Ops:
  0.0 153.4 %shard_map.37 = f32[768,512]{1,0:T(8,128)} custom-call(f32[24,16,768]{2,1,0:T(8,128)} %bitcast.1, f32[3,256,256]{2,1,0:T(8,128)} %inverses.1, f32[768,512]{1,0:T(8,128)} %right.1), custom_call_target="tpu_custom_call" | custom-call | tf_op jit(solution)/shard_map/pallas_call | solution.py:622
  153.4 2.7 %copy.5 = f32[768,512]{1,0:T(8,128)} copy(f32[768,512]{1,0:T(8,128)} %shard_map.37) | data formatting | bytes 3145728

commit v5 on v4

--- a/solution.py
+++ b/solution.py
@@ -8,10 +8,12 @@
 from jax.sharding import PartitionSpec as P
 
 MESH = pl.DeviceIdType.MESH
-CHUNKS = 8
-LEAD = 3
-BEHIND2 = 4
-BEHIND3 = 2
+CHUNKS = 16
+LEAD = 5
+KEPT3 = 1
+TAKE = (1, 2, 1, 0)
+BEHIND2 = 8
+BEHIND3 = 8
 F32, BF16 = jnp.float32, jnp.bfloat16
 
 
@@ -48,7 +50,7 @@
     per = max(1, 128 // width)
     up_z, down_z = (z + 1) % 4, (z + 3) % 4
     right_x, left_x = (x + 1) % 4, (x + 3) % 4
-    kept = jnp.where(x == 0, 3, jnp.where(x == 3, 1, 2))
+    kept = jnp.where(x == 3, KEPT3, 2)
 
     def place(group_, x_, yh_, z_, core_):
         return (group_ * 4 + x_, (yh_ * 4 + z_) * 2 + core_)
@@ -286,13 +288,19 @@
         def _():
             forward_x(j, c, 1).start()
 
-    step = n // 4
+    unit = max(1, n // 8)
+    taken = sum(TAKE) * unit
 
     def early_group(v):
         @pl.when(jnp.logical_and(is_a, x == 3))
         def _():
-            for k in range(step):
-                got_x(0, v * step + k)
+            for at, take in enumerate(TAKE):
+                first = sum(TAKE[:at]) * unit
+
+                @pl.when(v == at)
+                def _(first=first, take=take):
+                    for k in range(take * unit):
+                        got_x(0, first + k)
 
     def early_x(i):
         @pl.when(jnp.logical_and(jnp.logical_and(is_b, x == 3), i + LEAD < n))
@@ -304,6 +312,10 @@
 
             got_x(0, i + LEAD)
 
+        @pl.when(jnp.logical_and(jnp.logical_and(is_a, x == 3), i + taken < n))
+        def _():
+            got_x(0, i + taken)
+
         @pl.when(jnp.logical_and(jnp.logical_and(is_b, x == 0), jnp.logical_and(i >= 3, i % 2 == 0)))
         def _():
             got_x(1, i - 3)
@@ -318,19 +330,23 @@
     def send_sum(c):
         return remote(sums.at[c], sums.at[c], send_s.at[c], recv_s.at[c], cross)
 
-    def update(c, j):
-        hi, lo = split(xb[j, c])
+    def update(c, j, m):
+        hi, lo = split(xb[j, pl.ds(c, m)].reshape(m * width, block))
         both = jnp.concatenate([hi, lo], axis=0)
         for t in range(3):
             at = slice(t * panel, (t + 1) * panel)
             first = dot(both, lh[j, :, at])
-            res[c, :, at] -= first[:width] + (first[width:] + dot(hi, ll[j, :, at]))
+            value = first[: m * width] + (first[m * width :] + dot(hi, ll[j, :, at]))
+            res[pl.ds(c, m), :, at] -= value.reshape(m, width, panel)
 
     def solve(c):
         @pl.when(is_b)
         def _():
-            remote(sums.at[c], sums.at[c], send_s.at[c], recv_s.at[c], cross).wait_recv()
-            res[c] = res[c] - sums[c]
+            @pl.when(c % 2 == 0)
+            def _():
+                send_sum(c // 2).wait_recv()
+
+            res[c] = res[c] - sums[c // 2, pl.ds(pl.multiple_of(c % 2 * width, width), width)]
 
         one, two = slice(panel, 2 * panel), slice(2 * panel, 3 * panel)
         x0 = mult(res[c, :, :panel], ih[0], il[0])
@@ -414,47 +430,59 @@
 
     def own_group(v, carry):
         own_all(v)
-        own_near(v + 2)
-        own_far(v + 1)
-
-        @pl.when(jnp.logical_and(is_a, v == x - 1))
-        def _():
-            lax.fori_loop(0, kept, pass_on_cross, 0)
-
-        by_kind(v, lambda: finish(v, 1), lambda: finish(v), lambda: finish(v))
+
+        @pl.when(v > 0)
+        def _():
+            finish(v - 1)
+
         early_group(v)
         return carry
 
-    own_near(0)
-    own_near(1)
-    own_far(0)
+    def near_group(u, carry):
+        own_near(u)
+        return carry
+
+    def far_group(u, carry):
+        own_far(u)
+        return carry
+
+    lax.fori_loop(0, x + 1, near_group, 0)
+    lax.fori_loop(0, x + 1, far_group, 0)
+
+    @pl.when(jnp.logical_and(is_a, x > 0))
+    def _():
+        lax.fori_loop(0, kept, pass_on_cross, 0)
+
     lax.fori_loop(0, x + 1, own_group, 0)
+    finish(x, 1)
 
     ahead = jnp.where(x == 1, 2, 0)
     behind = jnp.where(x == 3, BEHIND3, jnp.where(x == 2, BEHIND2, n))
 
-    def total(c, carry):
-        @pl.when(jnp.logical_and(x == 1, c + ahead < n))
-        def _():
-            got_x(x + 1, c + ahead)
+    def total(m, carry):
+        for k in range(2):
+
+            @pl.when(jnp.logical_and(x == 1, 2 * m + k + ahead < n))
+            def _(k=k):
+                got_x(x + 1, 2 * m + k + ahead)
 
         def term(j, carry):
             @pl.when(jnp.logical_and(j > x, jnp.logical_or(x >= 2, j > x + 1)))
             def _():
-                got_x(j, c)
-
-            hi, lo = split(xb[j, c])
+                got_x(j, 2 * m)
+                got_x(j, 2 * m + 1)
+
+            hi, lo = split(xb[j, pl.ds(2 * m, 2)].reshape(2 * width, block))
             both = jnp.concatenate([hi, lo], axis=0)
             for t in range(3):
                 at = slice(t * panel, (t + 1) * panel)
                 first = dot(both, lh[4 + j, :, at])
-                value = first[:width] + (first[width:] + dot(hi, ll[4 + j, :, at]))
-                sums[c, :, at] = jnp.where(j == 0, 0.0, sums[c, :, at]) + value
+                value = first[: 2 * width] + (first[2 * width :] + dot(hi, ll[4 + j, :, at]))
+                sums[m, :, at] = jnp.where(j == 0, 0.0, sums[m, :, at]) + value
             return carry
 
         lax.fori_loop(0, 4, term, 0)
-        send_sum(c).start()
-
+        send_sum(m).start()
         return carry
 
     def close_all():
@@ -465,13 +493,19 @@
         early_x(c)
 
         def earlier(j, carry):
-            @pl.when(j < x)
+            @pl.when(j == x - 1)
+            def _():
+                got_x(j, c)
+                update(c, j, 1)
+
+            @pl.when(jnp.logical_and(j < x - 1, c % 2 == 0))
             def _():
                 @pl.when(jnp.logical_not(early(j)))
                 def _():
                     got_x(j, c)
-
-                update(c, j)
+                    got_x(j, c + 1)
+
+                update(c, j, 2)
 
             return carry
 
@@ -488,7 +522,9 @@
             def _():
                 close_all()
 
-            total(c - behind, 0)
+            @pl.when((c - behind) % 2 == 1)
+            def _():
+                total((c - behind) // 2, 0)
 
         return carry
 
@@ -520,7 +556,7 @@
         def _():
             close_all()
 
-        lax.fori_loop(n - behind, n, total, 0)
+        lax.fori_loop((n - behind) // 2, n // 2, total, 0)
 
     def sent_ring(slot, k=3):
         for a in range(2):
@@ -601,9 +637,9 @@
         def _():
             forward_x(x, c, 1).wait_send()
 
-        @pl.when(is_a)
-        def _():
-            send_sum(c).wait_send()
+        @pl.when(jnp.logical_and(is_a, c % 2 == 0))
+        def _():
+            send_sum(c // 2).wait_send()
 
         return carry
 
@@ -630,7 +666,7 @@
             pltpu.VMEM((8, block, block), BF16),
             pltpu.VMEM((4, n, width, block), F32),
             pltpu.VMEM((n, width, block), F32),
-            pltpu.VMEM((n, width, block), F32),
+            pltpu.VMEM((n // 2, 2 * width, block), F32),
             pltpu.VMEM((3, panel, panel), BF16),
             pltpu.VMEM((3, panel, panel), BF16),
             dma((6,)),

time: 156 us -> 152 us (0.974)
  Pallas kernels: 153 us -> 149 us
    pallas_call x1, Pallas kernels: 153 us -> 149 us  [body(): pl.pallas_call(functools.partial(kernel, n), out_shape=jax.ShapeDtypeStru...]
where the time goes in v5:
time: 152 us
  Pallas kernels  149 us (98%)
  local copies, waits for them, and re-layouts  2.67 us (2%)
    pallas_call x1, Pallas kernels, body(): pl.pallas_call(functools.partial(kernel, n), out_shape=jax.ShapeDtypeStru...  149 us

profile of v5, /device:TPU:14, one launch (start us, length us, event | category | flops | bytes accessed | tf_op | source)
XLA Modules:
  0.0 151.9 jit_solution(3623502866662104262)
XLA Ops:
  0.0 149.2 %shard_map.37 = f32[768,512]{1,0:T(8,128)} custom-call(f32[24,16,768]{2,1,0:T(8,128)} %bitcast.1, f32[3,256,256]{2,1,0:T(8,128)} %inverses.1, f32[768,512]{1,0:T(8,128)} %right.1), custom_call_target="tpu_custom_call" | custom-call | tf_op jit(solution)/shard_map/pallas_call | solution.py:658
  149.2 2.7 %copy.5 = f32[768,512]{1,0:T(8,128)} copy(f32[768,512]{1,0:T(8,128)} %shard_map.37) | data formatting | bytes 3145728

commit v6 on v5

--- a/solution.py
+++ b/solution.py
@@ -10,6 +10,8 @@
 MESH = pl.DeviceIdType.MESH
 CHUNKS = 16
 LEAD = 5
+FAR = 6
+AHEAD = 2
 KEPT3 = 1
 TAKE = (1, 2, 1, 0)
 BEHIND2 = 8
@@ -50,7 +52,7 @@
     per = max(1, 128 // width)
     up_z, down_z = (z + 1) % 4, (z + 3) % 4
     right_x, left_x = (x + 1) % 4, (x + 3) % 4
-    kept = jnp.where(x == 3, KEPT3, 2)
+    kept = jnp.where(x == 3, KEPT3, jnp.where(x == 0, 3, 2))
 
     def place(group_, x_, yh_, z_, core_):
         return (group_ * 4 + x_, (yh_ * 4 + z_) * 2 + core_)
@@ -264,15 +266,15 @@
         return jnp.logical_or(is_a, jnp.logical_or(x == 0, jnp.logical_and(x == 1, c % 2 == 1)))
 
     def far_east(c):
-        on_a = jnp.logical_or(x == 0, jnp.logical_and(x == 2, c < 2))
+        on_a = jnp.logical_or(jnp.logical_or(x == 0, jnp.logical_and(x == 3, c % 2 == 0)), jnp.logical_or(jnp.logical_and(x == 2, c < 2), jnp.logical_and(x == 1, c >= 8)))
         on_b = jnp.logical_and(x == 2, c % 2 == 0)
         return jnp.logical_or(jnp.logical_and(is_a, on_a), jnp.logical_and(is_b, on_b))
 
     def far_west(c):
-        on_a = jnp.logical_or(x == 1, jnp.logical_and(x == 0, c >= 2))
+        on_a = jnp.logical_or(jnp.logical_and(x == 1, c % 2 == 1), jnp.logical_and(x == 0, c >= 2))
         on_b = jnp.logical_and(x == 0, c % 2 == 1)
         either = jnp.logical_or(jnp.logical_and(is_a, on_a), jnp.logical_and(is_b, on_b))
-        return jnp.logical_or(x == 3, either)
+        return jnp.logical_or(jnp.logical_and(x == 3, jnp.logical_or(is_b, c < 8)), either)
 
     def forward_x(j, c, way):
         return remote(xb.at[j, c], xb.at[j, c], send_xf.at[c, way], recv_x.at[j, c], (east, west)[way])
@@ -320,9 +322,9 @@
         def _():
             got_x(1, i - 3)
 
-        @pl.when(jnp.logical_and(jnp.logical_and(is_a, x == 1), i >= n - 2))
-        def _():
-            got_x(2, i - (n - 2))
+        @pl.when(jnp.logical_and(jnp.logical_and(is_a, x == 1), i >= n - AHEAD))
+        def _():
+            got_x(2, i - (n - AHEAD))
 
     def early(j):
         return jnp.logical_and(x == 3, j == 0)
@@ -456,7 +458,7 @@
     lax.fori_loop(0, x + 1, own_group, 0)
     finish(x, 1)
 
-    ahead = jnp.where(x == 1, 2, 0)
+    ahead = jnp.where(x == 1, AHEAD, 0)
     behind = jnp.where(x == 3, BEHIND3, jnp.where(x == 2, BEHIND2, n))
 
     def total(m, carry):
@@ -512,9 +514,9 @@
         lax.fori_loop(0, x, earlier, 0)
         solve(c)
 
-        @pl.when(jnp.logical_and(jnp.logical_and(is_a, x > 0), jnp.logical_and(c % 2 == 1, c // 2 < kept)))
-        def _():
-            far_on(4 + c // 2)
+        @pl.when(jnp.logical_and(jnp.logical_and(is_a, x > 0), jnp.logical_and(c >= FAR, c - FAR < kept)))
+        def _():
+            far_on(4 + c - FAR)
 
         @pl.when(jnp.logical_and(is_a, c >= behind))
         def _():
@@ -552,7 +554,7 @@
             lax.fori_loop(0, n // 2, pass_second, 0)
             lax.fori_loop(kept - 1, kept, far_cross_group, 0)
 
-        @pl.when(x < 2)
+        @pl.when(behind == n)
         def _():
             close_all()
 

time: 152 us -> 152 us (level)
  no operation moved by 1% of the time
where the time goes in v6:
time: 152 us
  Pallas kernels  149 us (98%)
  local copies, waits for them, and re-layouts  2.67 us (2%)
    pallas_call x1, Pallas kernels, body(): pl.pallas_call(functools.partial(kernel, n), out_shape=jax.ShapeDtypeStru...  149 us

profile of v6, /device:TPU:14, one launch (start us, length us, event | category | flops | bytes accessed | tf_op | source)
XLA Modules:
  0.0 151.6 jit_solution(9002908706854359158)
XLA Ops:
  0.0 148.9 %shard_map.37 = f32[768,512]{1,0:T(8,128)} custom-call(f32[24,16,768]{2,1,0:T(8,128)} %bitcast.1, f32[3,256,256]{2,1,0:T(8,128)} %inverses.1, f32[768,512]{1,0:T(8,128)} %right.1), custom_call_target="tpu_custom_call" | custom-call | tf_op jit(solution)/shard_map/pallas_call | solution.py:660
  148.9 2.7 %copy.5 = f32[768,512]{1,0:T(8,128)} copy(f32[768,512]{1,0:T(8,128)} %shard_map.37) | data formatting | bytes 3145728

commit v7 on v6

--- a/solution.py
+++ b/solution.py
@@ -9,7 +9,7 @@
 
 MESH = pl.DeviceIdType.MESH
 CHUNKS = 16
-LEAD = 5
+LEAD = 4
 FAR = 6
 AHEAD = 2
 KEPT3 = 1

time: 152 us -> 152 us (level)
  no operation moved by 1% of the time
where the time goes in v7:
time: 152 us
  Pallas kernels  149 us (98%)
  local copies, waits for them, and re-layouts  2.67 us (2%)
    pallas_call x1, Pallas kernels, body(): pl.pallas_call(functools.partial(kernel, n), out_shape=jax.ShapeDtypeStru...  149 us

profile of v7, /device:TPU:14, one launch (start us, length us, event | category | flops | bytes accessed | tf_op | source)
XLA Modules:
  0.0 151.6 jit_solution(6001891465679922324)
XLA Ops:
  0.0 148.9 %shard_map.37 = f32[768,512]{1,0:T(8,128)} custom-call(f32[24,16,768]{2,1,0:T(8,128)} %bitcast.1, f32[3,256,256]{2,1,0:T(8,128)} %inverses.1, f32[768,512]{1,0:T(8,128)} %right.1), custom_call_target="tpu_custom_call" | custom-call | tf_op jit(solution)/shard_map/pallas_call | solution.py:660
  148.9 2.7 %copy.5 = f32[768,512]{1,0:T(8,128)} copy(f32[768,512]{1,0:T(8,128)} %shard_map.37) | data formatting | bytes 3145728
